TPU v7x, 256 devices: a whole 4x4x8 slice. The times are simulated.
256 devices in a mesh: mom: 8 (over z_lo, x), pts: 32 (over y, z_hi, core).
Axes of the slice: x: 4, y: 4, z: 8 (z_hi: 4, z_lo: 2; z = z_hi * 2 + z_lo), core: 2. Of those that a mesh axis runs over, the one named last changes fastest.
Arguments:
- amplitudes: bfloat16 [2, 2, 1, 256, 64, 128], P(None, None, None, 'mom'), may hold values from -6 to 6
- val_orbitals: bfloat16 [2, 256, 64, 512], P(None, 'mom'), may hold values from -0.25 to 0.25
- cond_orbitals: bfloat16 [2, 256, 512, 128], P(None, 'mom', 'pts'), may hold values from -0.25 to 0.25
- screened: bfloat16 [2, 256, 512, 512], P(None, None, ('pts', 'mom')), may hold values from -12 to 12
- val_energy: float32 [256, 64], P('mom', 'pts'), may hold values from -2 to -0.5
- cond_energy: float32 [256, 128], P('mom'), may hold values from 0.5 to 2
- grid_of_slot: int32 [256], replicated, may hold values from 0 to 255, as said below
- opposite_slot: int32 [256], P('mom'), may hold values from 0 to 255, as said below
Outputs:
- applied: float32 [2, 2, 1, 256, 64, 128], P(None, None, None, 'mom', 'pts')
Inputs may be any that keep to these rules, and one draw needn't show every extreme that they name: `grid_of_slot`: a permutation of the grid indices. opposite_slot[s] is the slot whose grid index is 255 - grid_of_slot[s]; it is never s, and s and opposite_slot[s] lie in aligned blocks of 32 slots whose first slots differ by 128.
All inputs are finite; a program needn't handle non-finite values.
Results may differ from a plain program's by a relative error of at most 0.006.
Values may be sent and summed in bfloat16 or wider, within the bound.
A program may use at most 128 MiB of HBM per device.

v0:
```python
import math
import jax
import jax.numpy as jnp
from jax import lax
from jax.sharding import PartitionSpec as P


def partner_2(value, axis, apart):
    mask = 2**apart
    pairs = [(source, source ^ mask) for source in range(lax.axis_size(axis))]
    return lax.ppermute(value, axis, pairs)


def complex_mix(formula, left, right, left_sign, right_sign):
    real_real = jnp.einsum(formula, left[0], right[0], preferred_element_type=jnp.float32)
    imag_imag = jnp.einsum(formula, left[1], right[1], preferred_element_type=jnp.float32)
    real_imag = jnp.einsum(formula, left[0], right[1], preferred_element_type=jnp.float32)
    imag_real = jnp.einsum(formula, left[1], right[0], preferred_element_type=jnp.float32)
    return jnp.stack(
        [
            real_real - left_sign * right_sign * imag_imag,
            right_sign * real_imag + left_sign * imag_real,
        ]
    )


def on_device(
    amplitudes,
    val_orbitals,
    cond_orbitals,
    screened,
    val_energy,
    cond_energy,
    grid_of_slot,
    opposite_slot,
):
    slots_here = opposite_slot.shape[0]
    total_slots = grid_of_slot.shape[0]
    rows_here = val_energy.shape[1]
    frequency = jnp.arange(total_slots, dtype=jnp.int32)
    phases = frequency[:, None] * grid_of_slot[None, :] % total_slots
    angles = phases.astype(jnp.float32) * (2.0 * math.pi / total_slots)
    cosine_table = jnp.cos(angles).astype(jnp.bfloat16)
    sine_table = jnp.sin(angles).astype(jnp.bfloat16)
    half_product = complex_mix("bnkvc,kuc->bnkvu", amplitudes, cond_orbitals, 1.0, 1.0).astype(
        jnp.bfloat16
    )
    pair_values = complex_mix("bnkvu,kvm->bnkum", half_product, val_orbitals, 1.0, -1.0).astype(
        jnp.bfloat16
    )
    flattened = pair_values.reshape(pair_values.shape[:4] + (-1,))
    weights = screened.reshape(2, total_slots, -1)
    inverse_count = 1.0 / total_slots
    whole_k = lax.all_to_all(flattened, "mom", split_axis=4, concat_axis=3, tiled=True)
    spec_real = jnp.einsum(
        "fs,bnsc->bnfc", cosine_table, whole_k[0], preferred_element_type=jnp.float32
    ) + jnp.einsum("fs,bnsc->bnfc", sine_table, whole_k[1], preferred_element_type=jnp.float32)
    spec_imag = jnp.einsum(
        "fs,bnsc->bnfc", cosine_table, whole_k[1], preferred_element_type=jnp.float32
    ) - jnp.einsum("fs,bnsc->bnfc", sine_table, whole_k[0], preferred_element_type=jnp.float32)
    prod_real = (weights[0] * spec_real - weights[1] * spec_imag).astype(jnp.bfloat16)
    prod_imag = (weights[0] * spec_imag + weights[1] * spec_real).astype(jnp.bfloat16)
    back_real = (
        jnp.einsum("fs,bnfc->bnsc", cosine_table, prod_real, preferred_element_type=jnp.float32)
        - jnp.einsum("fs,bnfc->bnsc", sine_table, prod_imag, preferred_element_type=jnp.float32)
    ) * inverse_count
    back_imag = (
        jnp.einsum("fs,bnfc->bnsc", cosine_table, prod_imag, preferred_element_type=jnp.float32)
        + jnp.einsum("fs,bnfc->bnsc", sine_table, prod_real, preferred_element_type=jnp.float32)
    ) * inverse_count
    field_pts = lax.all_to_all(
        jnp.stack([back_real, back_imag]).astype(jnp.bfloat16),
        "mom",
        split_axis=3,
        concat_axis=4,
        tiled=True,
    )
    field_pts = field_pts.reshape(pair_values.shape)
    weighted = complex_mix("bnkum,kvm->bnkvu", field_pts, val_orbitals, 1.0, 1.0).astype(
        jnp.bfloat16
    )
    band_terms = complex_mix("bnkvu,kuc->bnkvc", weighted, cond_orbitals, 1.0, -1.0)
    band_values = lax.psum_scatter(band_terms, "pts", scatter_dimension=4, tiled=True)
    top_bit = lax.axis_size("mom").bit_length() - 2
    partner = partner_2(band_values.astype(jnp.bfloat16), "mom", top_bit).astype(band_values.dtype)
    mirrored = jnp.take(partner, opposite_slot % slots_here, axis=3)
    start_row = lax.axis_index("pts") * rows_here
    own_rows = lax.dynamic_slice_in_dim(amplitudes, start_row, rows_here, 4).astype(jnp.float32)
    energy_gap = cond_energy[:, None, :] - val_energy[:, :, None]
    result_real = energy_gap * own_rows[0, 0] - band_values[0, 0] - mirrored[0, 1]
    result_imag = energy_gap * own_rows[1, 0] - band_values[1, 0] + mirrored[1, 1]
    anti_real = -energy_gap * own_rows[0, 1] + band_values[0, 1] + mirrored[0, 0]
    anti_imag = -energy_gap * own_rows[1, 1] + band_values[1, 1] - mirrored[1, 0]
    return jnp.stack([jnp.stack([result_real, anti_real]), jnp.stack([result_imag, anti_imag])])


def solution(mesh):
    in_specs = (
        P(None, None, None, "mom", None, None),
        P(None, "mom", None, None),
        P(None, "mom", "pts", None),
        P(None, None, ("pts", "mom"), None),
        P("mom", "pts"),
        P("mom", None),
        P(),
        P("mom"),
    )
    out_specs = P(None, None, None, "mom", "pts", None)
    return jax.shard_map(
        on_device, mesh=mesh, in_specs=in_specs, out_specs=out_specs, check_vma=False
    )
```

profile of v0, /device:TPU:2, one launch (start us, length us, event | category | flops | bytes accessed | tf_op | source)
XLA Modules:
  0.0 286.6 jit_solution(13320353008249521485)
XLA Ops:
  6.5 1.8 fusion.151
  8.3 0.9 fusion.65
  9.2 0.9 fusion.64
  10.2 0.9 fusion.55
  11.1 0.9 fusion.54
  12.0 0.4 fusion.10
  12.5 0.4 fusion.8
  12.9 0.4 fusion.24
  13.4 4.9 %copy.167 = bf16[2,1,32,16,512]{2,0,4,3,1:T(2,128)(2,1)} copy(bf16[2,1,32,16,512]{4,3,0,2,1:T(8,128)(2,1)S(1)} %fusion.24) | data formatting | bytes 2097152 | tf_op jit(solution)/shard_map/stack | solution.py:19
  18.3 2.1 fusion.27
  20.4 4.9 %copy.168 = bf16[2,1,32,16,512]{2,0,4,3,1:T(2,128)(2,1)} copy(bf16[2,1,32,16,512]{4,3,0,2,1:T(8,128)(2,1)S(1)} %fusion.27) | data formatting | bytes 2097152 | tf_op jit(solution)/shard_map/stack | solution.py:19
  25.3 16.3 %fusion.153 = bf16[8192,1,2,2,32]{4,3,2,1,0:T(2,128)(2,1)} fusion(bf16[1,2,1,32,8192]{3,1,0,2,4:T(2,128)(2,1)} %bitcast.313, bf16[1,2,1,32,8192]{3,1,0,2,4:T(2,128)(2,1)} %bitcast.312), kind=kLoop, calls=%fused_computation.180 | loop fusion | flops 1048576 | bytes 4194304
  41.7 11.2 %reshape.527 = bf16[8,2,65536]{2,1,0:T(2,128)(2,1)} reshape(bf16[8192,1,2,2,32]{4,3,2,1,0:T(2,128)(2,1)} %fusion.153) | data formatting | bytes 4194304
  52.9 6.3 %all-to-all-start = ((bf16[8,2,65536]{2,1,0:T(2,128)(2,1)}), bf16[8,2,65536]{2,1,0:T(2,128)(2,1)S(1)}, u32[]{:S(2)}, u32[]{:S(2)}) async-start(bf16[8,2,65536]{2,1,0:T(2,128)(2,1)} %reshape.527), calls=%async_computation | async-start | bytes 4194304 | tf_op jit(solution)/shard_map/all_to_all | solution.py:54
  59.2 2.1 slice_convert_fusion.1
  61.2 1.5 copy.166
  62.7 2.3 copy.170
  65.0 19.0 %all-to-all-done = bf16[8,2,65536]{2,1,0:T(2,128)(2,1)S(1)} async-done(((bf16[8,2,65536]{2,1,0:T(2,128)(2,1)}), bf16[8,2,65536]{2,1,0:T(2,128)(2,1)S(1)}, u32[]{:S(2)}, u32[]{:S(2)}) %all-to-all-start) | async-done | bytes 2097184 | tf_op jit(solution)/shard_map/all_to_all | solution.py:54
  84.0 6.5 %reshape.528 = bf16[8192,1,2,2,32]{4,3,2,1,0:T(2,128)(2,1)} reshape(bf16[8,2,65536]{2,1,0:T(2,128)(2,1)S(1)} %all-to-all-done) | data formatting | bytes 4194304
  90.6 11.9 %copy.169 = bf16[2,2,1,32,8,1024]{5,4,3,1,0,2:T(8,128)(2,1)S(1)} copy(bf16[2,2,1,32,8,1024]{3,1,0,5,4,2:T(2,128)(2,1)} %bitcast.311) | data formatting | bytes 4194304 | tf_op jit(solution)/shard_map/all_to_all | solution.py:54
  102.5 0.2 fusion.150
  102.7 0.6 copy.137
  103.3 0.6 copy.135
  103.8 1.4 fusion.92
  105.3 1.4 fusion.94
  106.7 1.4 convolution_subtract_fusion
  108.1 2.5 fusion.63
  110.6 1.4 fusion.90
  112.0 1.4 fusion.88
  113.3 1.4 fusion.30
  114.7 1.4 fusion.31
  116.1 0.2 pad_maximum_fusion.2
  116.3 4.1 %copy.142 = bf16[2,2,1,256,1024]{4,1,2,0,3:T(2,128)(2,1)} copy(bf16[2,2,1,256,1024]{3,4,1,2,0:T(8,128)(2,1)S(1)} %pad_maximum_fusion.2) | data formatting | bytes 4194304 | tf_op jit(solution)/shard_map/stack | solution.py:72
  120.4 30.3 %all_to_all.30 = bf16[2,2,1,256,1024]{4,1,2,0,3:T(2,128)(2,1)S(1)} all-to-all(bf16[2,2,1,256,1024]{4,1,2,0,3:T(2,128)(2,1)} %copy.142), channel_id=1, replica_groups=mesh['mom'=8,'pts'=32] {'mom'}, dimensions={3} | all-to-all | bytes 4194304 | tf_op jit(solution)/shard_map/all_to_all | solution.py:71
  150.8 0.6 copy.143
  151.4 1.2 fusion.149
  152.6 0.6 copy.145
  153.2 0.4 reshape.505
  153.6 3.2 %fusion.4 = f32[32,2,16,64]{3,2,1,0:T(8,128)} fusion(bf16[2,32,16,512]{3,2,0,1:T(8,128)(2,1)S(1)} %reshape.505, bf16[2,32,64,512]{3,2,1,0:T(8,128)(2,1)} %param.9), kind=kOutput, calls=%fused_computation.12 | convolution fusion | flops 67108864 | bytes 3407872 | tf_op jit(solution)/shard_map/bnkum,kvm->bnkvu/dot_general | solution.py:18
  156.7 0.6 copy.144
  157.3 0.4 reshape.504
  157.7 2.3 fusion.6
  160.0 2.3 fusion.56
  162.3 0.5 fusion.75
  162.8 0.5 fusion.79
  163.3 1.2 copy-done.1
  164.5 0.1 copy-done.6
  164.6 0.7 fusion.59
  165.2 0.5 subtract_bitcast_fusion
  165.7 0.5 add_bitcast_fusion
  166.2 0.6 pad_maximum_fusion.1
  166.8 4.4 %copy.146 = f32[2,2,1,32,64,128]{5,3,2,1,0,4:T(8,128)} copy(f32[2,2,1,32,64,128]{5,4,1,3,2,0:T(8,128)S(1)} %pad_maximum_fusion.1) | data formatting | bytes 8388608 | tf_op jit(solution)/shard_map/stack | solution.py:19
  171.2 0.6 copy-done.10
  172.0 1.0 dynamic-slice_convert_fusion
  173.0 99.4 %reduce-scatter.2.cloned.1.call-done = f32[2,2,1,32,2,128]{5,3,2,1,0,4:T(8,128)} async-done(((f32[2,2,1,32,64,128]{5,3,2,1,0,4:T(8,128)}), f32[2,2,1,32,2,128]{5,3,2,1,0,4:T(8,128)}) %reduce-scatter.2.cloned.1.call-update) | async-done | bytes 131088 | tf_op jit(solution)/shard_map/reduce_scatter | solution.py:83
  272.4 1.0 copy.199
  273.4 0.3 collective-permute-start
  273.7 0.8 fusion.152
  274.5 3.3 %collective-permute-done = bf16[2,2,1,32,2,128]{5,4,3,1,0,2:T(2,128)(2,1)S(1)} collective-permute-done((bf16[2,2,1,32,2,128]{5,4,3,1,0,2:T(2,128)(2,1)S(1)}, bf16[2,2,1,32,2,128]{5,4,3,1,0,2:T(2,128)(2,1)S(1)}, u32[]{:S(2)}, u32[]{:S(2)}) %collective-permute-start) | collective-permute-done | bytes 65568 | tf_op jit(solution)/shard_map/ppermute | solution.py:11
  277.8 0.7 gather_fusion
  278.6 0.1 bitcast_select_fusion
  278.7 0.1 fusion.108
  278.8 0.2 fusion.113
  279.1 0.7 maximum_bitcast_fusion
  (29 shorter events, 0.3 us)
Async XLA Ops:
  6.5 1.8 copy-start.4
  9.2 2.8 copy-start
  11.1 1.4 copy-start.5
  52.9 6.3 %copy-start.7 = (bf16[2,256,2,512]{3,2,1,0:T(2,128)(2,1)S(1)}, bf16[2,256,2,512]{3,2,1,0:T(2,128)(2,1)}, u32[]{:S(2)}) copy-start(bf16[2,256,2,512]{3,2,1,0:T(2,128)(2,1)} %param.11) | copy-start | bytes 3145732
  52.9 31.2 %all-to-all-start = ((bf16[8,2,65536]{2,1,0:T(2,128)(2,1)}), bf16[8,2,65536]{2,1,0:T(2,128)(2,1)S(1)}, u32[]{:S(2)}, u32[]{:S(2)}) async-start(bf16[8,2,65536]{2,1,0:T(2,128)(2,1)} %reshape.527), calls=%async_computation | async-start | bytes 4194304 | tf_op jit(solution)/shard_map/all_to_all | solution.py:54
  59.2 213.2 %reduce-scatter.2.cloned.1.call-start = ((), (), s32[]{:S(2)}) async-start(), calls=%async_computation.3 | async-start | bytes 4325376 | tf_op jit(solution)/shard_map/reduce_scatter | solution.py:83
  102.7 1.2 copy-start.9
  106.7 1.4 copy-start.2
  153.6 3.2 %copy-start.3 = (bf16[1,2,1,32,8,1024]{5,3,4,1,0,2:T(8,128)(2,1)S(1)}, bf16[1,2,1,32,8,1024]{5,3,4,1,0,2:T(8,128)(2,1)}, u32[]{:S(2)}) copy-start(bf16[1,2,1,32,8,1024]{5,3,4,1,0,2:T(8,128)(2,1)} %get-tuple-element.10) | copy-start | bytes 3145732
  162.3 2.2 copy-start.1
  162.3 2.3 copy-start.6
  171.2 0.7 copy-start.10
  171.2 0.8 copy-start.11
  171.2 107.5 %copy-start.8 = (f32[32,128]{1,0:T(8,128)S(1)}, f32[32,128]{1,0:T(8,128)}, u32[]{:S(2)}) copy-start(f32[32,128]{1,0:T(8,128)} %param.13) | copy-start | bytes 49156
  273.4 4.4 %collective-permute-start = (bf16[2,2,1,32,2,128]{5,4,3,1,0,2:T(2,128)(2,1)S(1)}, bf16[2,2,1,32,2,128]{5,4,3,1,0,2:T(2,128)(2,1)S(1)}, u32[]{:S(2)}, u32[]{:S(2)}) collective-permute-start(bf16[2,2,1,32,2,128]{5,4,3,1,0,2:T(2,128)(2,1)S(1)} %copy.199), channel_id=1, source_target_pairs={{0,128},{32,160},{64,192},{96,224},{128,0},{160,32},{192,64},{224,... | collective-permute-start | bytes 196616 | tf_op jit(solution)/shard_map/ppermute | solution.py:11
Sparse Core Ops, SparseCore 0:
  171.3 101.0 reduce-scatter.1
where the time goes:
time: 288 us; the launch traced here: 287 us
  waiting for transfers between devices  122 us (42%)
  local copies, waits for them, and re-layouts  63.2 us (22%)
  blocking collectives  30.3 us (11%)
  matrix products  29.7 us (10%)
  other arithmetic  21.4 us (7%)
  between operations  13.7 us (5%)
  starting transfers between devices  6.58 us (2%)
    reduce_scatter x1, waiting for transfers between devices, on_device(): lax.psum_scatter(band_terms, 'pts', scatter_dimension=4, tiled=True)  99.4 us
    all_to_all x1, blocking collectives, on_device(): lax.all_to_all(jnp.stack([back_real, back_imag]).astype(jnp.bfloat16), 'm...  30.3 us
    unnamed x27, local copies, waits for them, and re-layouts  19.8 us
    all_to_all x1, waiting for transfers between devices, on_device(): lax.all_to_all(flattened, 'mom', split_axis=4, concat_axis=3, tiled=True)  19 us
    unnamed x1, other arithmetic  16.3 us
    another operation x3, local copies, waits for them, and re-layouts, complex_mix(): jnp.stack([real_real - left_sign * right_sign * imag_imag, right_sign * r...  14.2 us
    all_to_all x1, local copies, waits for them, and re-layouts, on_device(): lax.all_to_all(flattened, 'mom', split_axis=4, concat_axis=3, tiled=True)  11.9 us
    all_to_all x1, starting transfers between devices, on_device(): lax.all_to_all(flattened, 'mom', split_axis=4, concat_axis=3, tiled=True)  6.32 us
  transfers between devices with their start and end apart: 3, of which 3 were waited for; matrix products, arithmetic and copies ran while one was open for 3% of the time, Pallas kernels for 0%

commit v1 on v0

--- a/solution.py
+++ b/solution.py
@@ -34,6 +34,19 @@
     grid_of_slot,
     opposite_slot,
 ):
+
+    def state_the_sectors(array_here, at_axis, dimension_no):
+        res = lax.psum(1, "mom")
+        return jnp.concatenate(
+            lax.all_to_all(
+                jnp.stack(jnp.split(array_here, res, at_axis)),
+                axis_name="mom",
+                split_axis=0,
+                concat_axis=0,
+            ),
+            dimension_no,
+        )
+
     slots_here = opposite_slot.shape[0]
     total_slots = grid_of_slot.shape[0]
     rows_here = val_energy.shape[1]
@@ -51,7 +64,7 @@
     flattened = pair_values.reshape(pair_values.shape[:4] + (-1,))
     weights = screened.reshape(2, total_slots, -1)
     inverse_count = 1.0 / total_slots
-    whole_k = lax.all_to_all(flattened, "mom", split_axis=4, concat_axis=3, tiled=True)
+    whole_k = state_the_sectors(flattened, 4, 3)
     spec_real = jnp.einsum(
         "fs,bnsc->bnfc", cosine_table, whole_k[0], preferred_element_type=jnp.float32
     ) + jnp.einsum("fs,bnsc->bnfc", sine_table, whole_k[1], preferred_element_type=jnp.float32)

time: 288 us -> 243 us (0.84)
  local copies, waits for them, and re-layouts: 63.2 us -> 33.7 us
  other arithmetic: 21.4 us -> 5.05 us
    unnamed x1 -> x0, other arithmetic: 16.3 us -> none
    unnamed x27 -> x33, local copies, waits for them, and re-layouts: 19.8 us -> 8.08 us
    all_to_all x1, local copies, waits for them, and re-layouts: 11.9 us -> 0.17 us  [state_the_sectors(): lax.all_to_all(jnp.stack(jnp.split(array_here, res, at_axis)), axis_name=...]
    another operation x3 -> x4, local copies, waits for them, and re-layouts: 14.2 us -> 8.63 us  [complex_mix(): jnp.stack([real_real - left_sign * right_sign * imag_imag, right_sign * r...]
where the time goes in v1:
time: 243 us
  waiting for transfers between devices  122 us (50%)
  local copies, waits for them, and re-layouts  33.7 us (14%)
  matrix products  31.4 us (13%)
  blocking collectives  30.3 us (12%)
  between operations  13.7 us (6%)
  starting transfers between devices  6.6 us (3%)
  other arithmetic  5.05 us (2%)
    reduce_scatter x1, waiting for transfers between devices, on_device(): lax.psum_scatter(band_terms, 'pts', scatter_dimension=4, tiled=True)  99.5 us
    all_to_all x1, blocking collectives, on_device(): lax.all_to_all(jnp.stack([back_real, back_imag]).astype(jnp.bfloat16), 'm...  30.3 us
    all_to_all x1, waiting for transfers between devices, state_the_sectors(): lax.all_to_all(jnp.stack(jnp.split(array_here, res, at_axis)), axis_name=...  19.1 us
    another operation x4, local copies, waits for them, and re-layouts, complex_mix(): jnp.stack([real_real - left_sign * right_sign * imag_imag, right_sign * r...  8.63 us
    unnamed x33, local copies, waits for them, and re-layouts  8.08 us
    dot_general x4, matrix products, complex_mix(): jnp.einsum(formula, left[1], right[1], preferred_element_type=jnp.float32)  6.83 us
    all_to_all x1, starting transfers between devices, state_the_sectors(): lax.all_to_all(jnp.stack(jnp.split(array_here, res, at_axis)), axis_name=...  6.32 us
    dot_general x4, matrix products, complex_mix(): jnp.einsum(formula, left[1], right[0], preferred_element_type=jnp.float32)  5.03 us
  transfers between devices with their start and end apart: 3, of which 3 were waited for; matrix products, arithmetic and copies ran while one was open for 3% of the time, Pallas kernels for 0%

profile of v1, /device:TPU:2, one launch (start us, length us, event | category | flops | bytes accessed | tf_op | source)
XLA Modules:
  0.0 242.8 jit_solution(7582735988392443048)
XLA Ops:
  6.5 1.8 fusion.159
  8.3 0.9 fusion.64
  9.2 0.9 fusion.65
  10.2 0.9 fusion.54
  11.1 0.9 fusion.55
  12.0 0.4 fusion.8
  12.5 0.4 fusion.10
  12.9 1.4 fusion.27
  14.4 1.8 stack.80
  16.2 3.1 %fusion.24 = bf16[2,1,32,16,512]{4,3,0,2,1:T(8,128)(2,1)} fusion(f32[32,2,16,512]{3,2,1,0:T(8,128)S(1)} %fusion.10, bf16[2,32,64,16]{2,3,0,1:T(8,128)(2,1)} %copy-done.5, bf16[2,32,64,512]{3,2,1,0:T(8,128)(2,1)} %param.9), kind=kOutput, calls=%fused_computation.36 | convolution fusion | flops 68681728 | bytes 5505024 | tf_op jit(solution)/shard_map/bnkvu,kvm->bnkum/dot_general | solution.py:16
  19.3 1.8 stack.79
  21.2 0.6 copy_dynamic-update-slice_fusion.1
  21.8 0.6 copy_dynamic-update-slice_fusion
  22.4 0.7 fusion.76
  23.1 0.7 fusion.75
  23.8 0.7 fusion.74
  24.5 0.7 fusion.73
  25.2 0.7 fusion.72
  25.9 0.7 fusion.71
  26.6 0.7 fusion.70
  27.4 0.7 fusion.69
  28.1 6.3 %all-to-all-start = ((bf16[8,2,2,1,32,1024]{5,4,2,3,1,0:T(8,128)(2,1)}), bf16[8,2,2,1,32,1024]{5,4,2,3,1,0:T(8,128)(2,1)S(1)}, u32[]{:S(2)}, u32[]{:S(2)}) async-start(bf16[8,2,2,1,32,1024]{5,4,2,3,1,0:T(8,128)(2,1)} %fusion.69), calls=%async_computation | async-start | bytes 4194304 | tf_op jit(solution)/shard_map/all_to_all | solution.py:41
  34.4 2.0 slice_convert_fusion.1
  36.4 1.5 copy.103
  37.9 2.3 copy.104
  40.2 19.1 %all-to-all-done = bf16[8,2,2,1,32,1024]{5,4,2,3,1,0:T(8,128)(2,1)S(1)} async-done(((bf16[8,2,2,1,32,1024]{5,4,2,3,1,0:T(8,128)(2,1)}), bf16[8,2,2,1,32,1024]{5,4,2,3,1,0:T(8,128)(2,1)S(1)}, u32[]{:S(2)}, u32[]{:S(2)}) %all-to-all-start) | async-done | bytes 2097184 | tf_op jit(solution)/shard_map/all_to_all | solution.py:41
  59.4 0.2 fusion.158
  59.7 0.4 copy-done.9
  60.1 1.4 fusion.100
  61.5 1.4 fusion.102
  63.0 1.4 convolution_subtract_fusion
  64.4 2.2 fusion.63
  66.6 1.4 fusion.98
  68.0 1.4 fusion.96
  69.4 1.4 fusion.30
  70.8 1.4 fusion.31
  72.4 4.1 %copy.79 = bf16[2,2,1,256,1024]{4,1,2,0,3:T(2,128)(2,1)} copy(bf16[2,2,1,256,1024]{3,4,1,2,0:T(8,128)(2,1)S(1)} %pad_maximum_fusion.1) | data formatting | bytes 4194304 | tf_op jit(solution)/shard_map/stack | solution.py:85
  76.5 30.3 %all_to_all.20 = bf16[2,2,1,256,1024]{4,1,2,0,3:T(2,128)(2,1)S(1)} all-to-all(bf16[2,2,1,256,1024]{4,1,2,0,3:T(2,128)(2,1)} %copy.79), channel_id=1, replica_groups=mesh['mom'=8,'pts'=32] {'mom'}, dimensions={3} | all-to-all | bytes 4194304 | tf_op jit(solution)/shard_map/all_to_all | solution.py:84
  106.8 0.6 copy.80
  107.5 1.2 fusion.157
  108.6 0.6 copy.82
  109.2 0.4 reshape.510
  109.6 3.2 %fusion.4 = f32[32,2,16,64]{3,2,1,0:T(8,128)} fusion(bf16[2,32,16,512]{3,2,0,1:T(8,128)(2,1)S(1)} %reshape.510, bf16[2,32,64,512]{3,2,1,0:T(8,128)(2,1)} %param.9), kind=kOutput, calls=%fused_computation.11 | convolution fusion | flops 67108864 | bytes 3407872 | tf_op jit(solution)/shard_map/bnkum,kvm->bnkvu/dot_general | solution.py:18
  112.8 0.6 copy.81
  113.4 0.4 reshape.509
  113.8 2.3 fusion.6
  116.0 2.3 fusion.56
  118.3 0.5 fusion.83
  118.8 0.5 fusion.87
  119.3 1.2 copy-done.1
  120.6 0.7 fusion.59
  121.3 0.5 subtract_bitcast_fusion
  121.8 0.5 add_bitcast_fusion
  122.3 0.6 pad_maximum_fusion
  122.9 4.4 %copy.83 = f32[2,2,1,32,64,128]{5,3,2,1,0,4:T(8,128)} copy(f32[2,2,1,32,64,128]{5,4,1,3,2,0:T(8,128)S(1)} %pad_maximum_fusion) | data formatting | bytes 8388608 | tf_op jit(solution)/shard_map/stack | solution.py:19
  127.3 0.6 copy-done.10
  128.0 1.0 dynamic-slice_convert_fusion
  129.0 99.5 %reduce-scatter.2.cloned.1.call-done = f32[2,2,1,32,2,128]{5,3,2,1,0,4:T(8,128)} async-done(((f32[2,2,1,32,64,128]{5,3,2,1,0,4:T(8,128)}), f32[2,2,1,32,2,128]{5,3,2,1,0,4:T(8,128)}) %reduce-scatter.2.cloned.1.call-update) | async-done | bytes 131088 | tf_op jit(solution)/shard_map/reduce_scatter | solution.py:96
  228.5 1.0 copy.136
  229.6 0.3 collective-permute-start
  229.8 0.8 fusion.160
  230.7 3.2 %collective-permute-done = bf16[2,2,1,32,2,128]{5,4,3,1,0,2:T(2,128)(2,1)S(1)} collective-permute-done((bf16[2,2,1,32,2,128]{5,4,3,1,0,2:T(2,128)(2,1)S(1)}, bf16[2,2,1,32,2,128]{5,4,3,1,0,2:T(2,128)(2,1)S(1)}, u32[]{:S(2)}, u32[]{:S(2)}) %collective-permute-start) | collective-permute-done | bytes 65568 | tf_op jit(solution)/shard_map/ppermute | solution.py:11
  234.0 0.7 gather_fusion
  235.2 0.7 maximum_bitcast_fusion
  (34 shorter events, 1.1 us)
Async XLA Ops:
  6.5 1.8 copy-start.4
  9.2 2.8 %copy-start = (bf16[2,32,64,512]{3,2,1,0:T(8,128)(2,1)S(1)}, bf16[2,32,64,512]{3,2,1,0:T(8,128)(2,1)}, u32[]{:S(2)}) copy-start(bf16[2,32,64,512]{3,2,1,0:T(8,128)(2,1)} %param.9) | copy-start | bytes 12582916
  11.1 1.4 copy-start.5
  28.1 6.3 %copy-start.7 = (bf16[2,256,2,512]{3,2,1,0:T(2,128)(2,1)S(1)}, bf16[2,256,2,512]{3,2,1,0:T(2,128)(2,1)}, u32[]{:S(2)}) copy-start(bf16[2,256,2,512]{3,2,1,0:T(2,128)(2,1)} %param.11) | copy-start | bytes 3145732
  28.1 31.2 %all-to-all-start = ((bf16[8,2,2,1,32,1024]{5,4,2,3,1,0:T(8,128)(2,1)}), bf16[8,2,2,1,32,1024]{5,4,2,3,1,0:T(8,128)(2,1)S(1)}, u32[]{:S(2)}, u32[]{:S(2)}) async-start(bf16[8,2,2,1,32,1024]{5,4,2,3,1,0:T(8,128)(2,1)} %fusion.69), calls=%async_computation | async-start | bytes 4194304 | tf_op jit(solution)/shard_map/all_to_all | solution.py:41
  34.4 194.1 %reduce-scatter.2.cloned.1.call-start = ((), (), s32[]{:S(2)}) async-start(), calls=%async_computation.3 | async-start | bytes 4325376 | tf_op jit(solution)/shard_map/reduce_scatter | solution.py:96
  59.4 0.7 copy-start.9
  62.9 1.4 copy-start.2
  109.6 3.2 %copy-start.3 = (bf16[1,2,1,32,8,1024]{5,3,4,1,0,2:T(8,128)(2,1)S(1)}, bf16[1,2,1,32,8,1024]{5,3,4,1,0,2:T(8,128)(2,1)}, u32[]{:S(2)}) copy-start(bf16[1,2,1,32,8,1024]{5,3,4,1,0,2:T(8,128)(2,1)} %get-tuple-element.10) | copy-start | bytes 3145732
  118.3 2.2 copy-start.1
  118.3 2.3 copy-start.6
  127.2 0.7 copy-start.10
  127.2 0.8 copy-start.11
  127.2 107.6 %copy-start.8 = (f32[32,128]{1,0:T(8,128)S(1)}, f32[32,128]{1,0:T(8,128)}, u32[]{:S(2)}) copy-start(f32[32,128]{1,0:T(8,128)} %param.13) | copy-start | bytes 49156
  229.6 4.4 %collective-permute-start = (bf16[2,2,1,32,2,128]{5,4,3,1,0,2:T(2,128)(2,1)S(1)}, bf16[2,2,1,32,2,128]{5,4,3,1,0,2:T(2,128)(2,1)S(1)}, u32[]{:S(2)}, u32[]{:S(2)}) collective-permute-start(bf16[2,2,1,32,2,128]{5,4,3,1,0,2:T(2,128)(2,1)S(1)} %copy.136), channel_id=1, source_target_pairs={{0,128},{32,160},{64,192},{96,224},{128,0},{160,32},{192,64},{224,... | collective-permute-start | bytes 196616 | tf_op jit(solution)/shard_map/ppermute | solution.py:11
Sparse Core Ops, SparseCore 0:
  127.4 101.1 reduce-scatter.1
